TPU v7x, 32 devices: a whole 2x2x4 slice. The times are simulated.
32 devices in a mesh: seg: 8 (over z, y), op: 4 (over x, core).
Axes of the slice: x: 2, y: 2, z: 4, core: 2. Of those that a mesh axis runs over, the one named last changes fastest.
Arguments:
- label_map: int32 [8, 16], P('seg'), may hold values from 0 to 15, each once within a row
- site_blocks: float32 [8, 16, 128, 128], P('seg'), may hold values from -0.25 to 1.25
- left_ops: bfloat16 [48, 16, 128, 128], P('op'), may hold values from -0.5 to 0.5
- right_ops: bfloat16 [8, 48, 16, 128, 128], P('seg', 'op'), may hold values from -0.078125 to 0.078125
- wavefunction: bfloat16 [8, 16, 128, 128], P('seg', 'op'), may hold values from -72 to 72
Outputs:
- ham_psi: bfloat16 [8, 16, 128, 128], P('seg', 'op')
- ham_squared_psi: bfloat16 [8, 16, 128, 128], P('seg', 'op')
Inputs may be any that keep to these rules, and one draw needn't show every extreme that they name: Each row of label_map is a permutation of 0 to 15.
All inputs are finite; a program needn't handle non-finite values.
Results may differ from a plain program's by a relative error of at most 0.022.
Values may be sent and summed in bfloat16 or wider, within the bound.
A program may use at most 128 MiB of HBM per device.

v0:
```python
import jax
import jax.numpy as jnp
from jax import lax
from jax.sharding import PartitionSpec as P


def shifted(array, axis, by):
    peers = lax.axis_size(axis)
    pairs = [(i, i + by) for i in range(peers) if 0 <= i + by < peers]
    return lax.ppermute(array, axis, pairs)


def on_device(label_map, site_blocks, left_ops, right_ops, wavefunction):
    highest = lax.Precision.HIGHEST
    sectors = site_blocks.shape[1]
    block_len = site_blocks.shape[2]
    groups = lax.axis_size("op")
    per_group = sectors // groups
    first_sector = lax.axis_index("op") * per_group
    sector_map = label_map[0]
    own_blocks = site_blocks[0]
    identity = jnp.eye(block_len, dtype=jnp.float32)
    anchor = first_sector + jnp.arange(per_group, dtype=jnp.int32)
    start_blocks = jnp.broadcast_to(identity, (per_group, block_len, block_len))
    start_labels = anchor.astype(jnp.float32)
    is_first = lax.axis_index("seg") == 0

    def relay_step(counter, state_pair):
        cur_blocks, cur_labels = state_pair
        current = cur_labels.astype(jnp.int32)
        next_blocks = jnp.einsum(
            "qij,qjk->qik", cur_blocks, jnp.take(own_blocks, current, axis=0), precision=highest
        )
        next_labels = jnp.take(sector_map, current).astype(jnp.float32)
        recv_blocks, recv_labels = shifted((next_blocks, next_labels), "seg", 1)
        return (
            jnp.where(is_first, start_blocks, recv_blocks),
            jnp.where(is_first, start_labels, recv_labels),
        )

    relayed = lax.fori_loop(0, lax.axis_size("seg") - 1, relay_step, (start_blocks, start_labels))
    prefix, prefix_labels = (
        lax.all_gather(relayed[0].astype(jnp.bfloat16), "op", axis=0, tiled=True).astype(
            jnp.float32
        ),
        lax.all_gather(relayed[1].astype(jnp.bfloat16), "op", axis=0, tiled=True).astype(
            jnp.float32
        ),
    )
    labels_int = prefix_labels.astype(jnp.int32)
    inverse = jnp.argsort(labels_int)
    inner_prod = jnp.einsum(
        "kqjl,qlm->kqjm", left_ops, prefix, precision=highest, preferred_element_type=jnp.float32
    )
    environ = jnp.einsum("qji,kqjm->kqim", prefix, inner_prod, precision=highest)
    environ = jnp.take(environ, inverse, axis=1).astype(jnp.bfloat16)
    right_local = right_ops[0]

    def apply_ham(portion):
        half_prod = jnp.einsum(
            "kpij,pjl->kpil", environ, portion, preferred_element_type=jnp.float32
        ).astype(jnp.bfloat16)
        return jnp.einsum(
            "kpil,kpml->pim", half_prod, right_local, preferred_element_type=jnp.float32
        )

    partial_sum = apply_ham(lax.all_gather(wavefunction[0], "op", axis=0, tiled=True))
    entries = sectors * block_len * block_len
    hpsi_sum = lax.psum(partial_sum.astype(jnp.bfloat16), "op").astype(jnp.float32)
    scale_fac = lax.rsqrt(jnp.sum(hpsi_sum * hpsi_sum) / entries + 1e-06)
    unit_vec = (hpsi_sum * scale_fac).astype(jnp.bfloat16)
    first_out = lax.dynamic_slice_in_dim(hpsi_sum, first_sector, per_group, 0).astype(jnp.bfloat16)
    second_part = apply_ham(unit_vec)
    second_out = lax.psum_scatter(
        second_part.astype(jnp.bfloat16), "op", scatter_dimension=0, tiled=True
    )
    return (first_out[None], second_out[None])


def solution(mesh):
    in_specs = (
        P("seg", None),
        P("seg", None, None, None),
        P("op", None, None, None),
        P("seg", "op", None, None, None),
        P("seg", "op", None, None),
    )
    out_specs = (P("seg", "op", None, None), P("seg", "op", None, None))
    return jax.shard_map(
        on_device, mesh=mesh, in_specs=in_specs, out_specs=out_specs, check_vma=False
    )
```

profile of v0, /device:TPU:29, one launch (start us, length us, event | category | flops | bytes accessed | tf_op | source)
XLA Modules:
  0.0 226.6 jit_solution(12428908099538541725)
XLA Ops:
  7.3 84.1 %while.13 = (s32[]{:T(128)}, f32[4,128,128]{1,2,0:T(8,128)S(1)}, f32[4]{0:T(128)S(1)}, pred[]{:T(512)}, f32[16,128,128]{2,1,0:T(8,128)}, /*index=5*/s32[16]{0:T(128)}, f32[128,128]{0,1:T(8,128)S(1)}, s32[]{:T(128)}, s32[]{:T(128)}) while((s32[]{:T(128)}, f32[4,128,128]{1,2,0:T(8,128)S(1)}, f32[4]{0:T(128)S(1)}, pred[]{:T(512)}, ...), condition=%wide.region_1.0_spmd.clone, body=%wide.region_0.1_spmd.clone.sunk | while | flops 100795456 | bytes 2953659 | solution.py:41
  7.3 1.3 gather_fusion.1
  8.6 1.8 gather_fusion
  13.7 6.5 %collective-permute-done.1 = f32[4]{0:T(128)S(1)} collective-permute-done((f32[4]{0:T(128)S(1)}, f32[4]{0:T(128)S(1)}, u32[]{:S(2)}, u32[]{:S(2)}) %collective-permute-start.1) | collective-permute-done | bytes 48 | tf_op jit(solution)/shard_map/while/body/eval_jaxpr/ppermute | solution.py:10
  20.3 1.3 gather_fusion.1
  21.6 1.8 gather_fusion
  26.6 5.5 %collective-permute-done.1 = f32[4]{0:T(128)S(1)} collective-permute-done((f32[4]{0:T(128)S(1)}, f32[4]{0:T(128)S(1)}, u32[]{:S(2)}, u32[]{:S(2)}) %collective-permute-start.1) | collective-permute-done | bytes 48 | tf_op jit(solution)/shard_map/while/body/eval_jaxpr/ppermute | solution.py:10
  32.2 1.3 gather_fusion.1
  33.5 1.8 gather_fusion
  38.6 5.1 %collective-permute-done.1 = f32[4]{0:T(128)S(1)} collective-permute-done((f32[4]{0:T(128)S(1)}, f32[4]{0:T(128)S(1)}, u32[]{:S(2)}, u32[]{:S(2)}) %collective-permute-start.1) | collective-permute-done | bytes 48 | tf_op jit(solution)/shard_map/while/body/eval_jaxpr/ppermute | solution.py:10
  43.8 1.3 gather_fusion.1
  45.1 1.8 gather_fusion
  50.1 5.5 %collective-permute-done.1 = f32[4]{0:T(128)S(1)} collective-permute-done((f32[4]{0:T(128)S(1)}, f32[4]{0:T(128)S(1)}, u32[]{:S(2)}, u32[]{:S(2)}) %collective-permute-start.1) | collective-permute-done | bytes 48 | tf_op jit(solution)/shard_map/while/body/eval_jaxpr/ppermute | solution.py:10
  57.0 1.8 gather_fusion
  62.1 5.5 %collective-permute-done.1 = f32[4]{0:T(128)S(1)} collective-permute-done((f32[4]{0:T(128)S(1)}, f32[4]{0:T(128)S(1)}, u32[]{:S(2)}, u32[]{:S(2)}) %collective-permute-start.1) | collective-permute-done | bytes 48 | tf_op jit(solution)/shard_map/while/body/eval_jaxpr/ppermute | solution.py:10
  67.6 1.3 gather_fusion.1
  68.9 1.8 gather_fusion
  74.0 5.5 %collective-permute-done.1 = f32[4]{0:T(128)S(1)} collective-permute-done((f32[4]{0:T(128)S(1)}, f32[4]{0:T(128)S(1)}, u32[]{:S(2)}, u32[]{:S(2)}) %collective-permute-start.1) | collective-permute-done | bytes 48 | tf_op jit(solution)/shard_map/while/body/eval_jaxpr/ppermute | solution.py:10
  80.9 1.8 gather_fusion
  85.9 5.5 %collective-permute-done.1 = f32[4]{0:T(128)S(1)} collective-permute-done((f32[4]{0:T(128)S(1)}, f32[4]{0:T(128)S(1)}, u32[]{:S(2)}, u32[]{:S(2)}) %collective-permute-start.1) | collective-permute-done | bytes 48 | tf_op jit(solution)/shard_map/while/body/eval_jaxpr/ppermute | solution.py:10
  93.0 13.1 %all-reduce = bf16[16]{0:T(256)(128)(2,1)S(1)} all-reduce(bf16[16]{0:T(256)(128)(2,1)S(1)} %dynamic-update-slice), channel_id=1, replica_groups=mesh['seg'=8,'op'=4] {'op'}, use_global_device_ids=true, to_apply=%add | all-reduce | flops 16 | bytes 64
  107.4 7.9 %all_gather.10 = bf16[16,128,128]{2,1,0:T(8,128)(2,1)S(1)} all-gather(bf16[4,128,128]{2,1,0:T(8,128)(2,1)S(1)} %copy.19), channel_id=1, replica_groups=mesh['seg'=8,'op'=4] {'op'}, dimensions={0}, use_global_device_ids=true | all-gather | bytes 655360 | tf_op jit(solution)/shard_map/all_gather | solution.py:43
  115.3 4.6 %fusion.15 = f32[16,128,12,128]{3,1,2,0:T(8,128)S(1)} fusion(bf16[12,16,128,128]{3,2,1,0:T(8,128)(2,1)} %param.9, bf16[16,128,128]{2,1,0:T(8,128)(2,1)S(1)} %all_gather.10), kind=kOutput, calls=%fused_computation.24 | convolution fusion | flops 805306368 | bytes 19398656 | tf_op jit(solution)/shard_map/kqjl,qlm->kqjm/dot_general | solution.py:52
  120.0 7.9 %fusion.23 = bf16[12,16,128,128]{2,3,0,1:T(8,128)(2,1)} fusion(f32[16,128,12,128]{3,1,2,0:T(8,128)S(1)} %fusion.15, bf16[16,128,128]{2,1,0:T(8,128)(2,1)S(1)} %all_gather.10), kind=kOutput, calls=%fused_computation.31 | convolution fusion | flops 4831838208 | bytes 19398656 | tf_op jit(solution)/shard_map/qji,kqjm->kqim/dot_general | solution.py:55
  127.9 7.3 %all-gather = bf16[1,16,128,128]{3,2,0,1:T(8,128)(2,1)S(1)} all-gather(bf16[1,4,128,128]{3,2,0,1:T(8,128)(2,1)S(1)} %bitcast.83), channel_id=2, replica_groups=mesh['seg'=8,'op'=4] {'op'}, dimensions={1}, use_global_device_ids=true | all-gather | bytes 655360 | tf_op jit(solution)/shard_map/all_gather | solution.py:67
  135.2 6.8 %gather_fusion.2 = bf16[16,12,128,128]{2,3,1,0:T(8,128)(2,1)} fusion(bf16[12,16,128,128]{2,3,0,1:T(8,128)(2,1)} %fusion.23, s32[1024]{0:T(1024)S(1)} %pad_clamp_fusion.1), kind=kCustom, calls=%fused_computation.2 | custom fusion | bytes 12582976 | tf_op jit(solution)/shard_map/jit(_take)/gather | solution.py:56
  142.0 9.4 %fusion.38 = bf16[16,128,128]{2,1,0:T(8,128)(2,1)} fusion(bf16[1,16,128,128]{3,2,0,1:T(8,128)(2,1)S(1)} %all-gather, bf16[16,12,128,128]{2,3,1,0:T(8,128)(2,1)} %gather_fusion.2, pred[16]{0:T(512)(128)(4,1)S(1)} %compare_and_fusion.1, bf16[1,12,16,128,128]{4,3,2,1,0:T(8,128)(2,1)} %param.10), kind=kOutput, calls=%fused_computation.35 | convolution fusion | flops 1617166336 | bytes 13631504 | tf_op jit(solution)/shard_map/kpil,kpml->pim/dot_general | solution.py:63
  151.6 33.5 %all-reduce.3.cloned.1.call-done = bf16[16,128,128]{2,1,0:T(8,128)(2,1)} async-done(((bf16[16,128,128]{2,1,0:T(8,128)(2,1)}), bf16[16,128,128]{2,1,0:T(8,128)(2,1)}) %all-reduce.3.cloned.1.call-update) | async-done | bytes 524304 | tf_op jit(solution)/shard_map/psum | solution.py:69
  185.1 1.9 multiply_reduce_fusion
  187.7 9.3 %fusion.43 = bf16[16,128,128]{2,1,0:T(8,128)(2,1)} fusion(f32[]{:T(128)S(6)} %rsqrt.3, bf16[16,128,128]{2,1,0:T(8,128)(2,1)} %all-reduce.3.cloned.1.call-done, bf16[16,12,128,128]{2,3,1,0:T(8,128)(2,1)} %gather_fusion.2, pred[16]{0:T(512)(128)(4,1)S(1)} %compare_and_fusion.1, bf16[1,12,16,128,128]{4,3,2,1,0:T(8,128)(2,1)} %param.10), kind=kOutput, calls=%fused_computation.36 | convolution fusion | flops 1617952768 | bytes 13631508 | tf_op jit(solution)/shard_map/kpil,kpml->pim/dot_general | solution.py:63
  197.0 1.6 fusion.59
  198.6 21.1 %reduce-scatter.2.cloned.1.call-done = bf16[4,128,128]{2,1,0:T(8,128)(2,1)} async-done(((bf16[16,128,128]{2,1,0:T(8,128)(2,1)}), bf16[4,128,128]{2,1,0:T(8,128)(2,1)}) %reduce-scatter.2.cloned.1.call-update) | async-done | bytes 131088 | tf_op jit(solution)/shard_map/reduce_scatter | solution.py:74
  (87 shorter events, 28.3 us)
Async XLA Ops:
  7.2 177.9 %all-reduce.3.cloned.1.call-start = ((), (), s32[]{:S(2)}) async-start(), calls=%async_computation.1 | async-start | bytes 1048576 | tf_op jit(solution)/shard_map/psum | solution.py:69
  7.3 84.2 %copy-start.1 = (u32[32]{0:T(128)S(1)}, u32[32]{0:T(128)}, u32[]{:S(2)}) copy-start(u32[32]{0:T(128)} %constant.75) | copy-start | bytes 388
  11.1 9.1 %collective-permute-start = (f32[4,128,128]{1,2,0:T(8,128)S(1)}, f32[4,128,128]{1,2,0:T(8,128)S(1)}, u32[]{:S(2)}, u32[]{:S(2)}) collective-permute-start(f32[4,128,128]{1,2,0:T(8,128)S(1)} %convolution_bitcast_fusion.2), channel_id=1, source_target_pairs={{0,4},{4,8},{8,12},{12,16},{16,20},{20,24},{24,28},{1,5},{5,9},{9,... | collective-permute-start | bytes 786440 | tf_op jit(solution)/shard_map/while/body/eval_jaxpr/ppermute | solution.py:10
  12.4 7.8 %collective-permute-start.1 = (f32[4]{0:T(128)S(1)}, f32[4]{0:T(128)S(1)}, u32[]{:S(2)}, u32[]{:S(2)}) collective-permute-start(f32[4]{0:T(128)S(1)} %get-tuple-element.140), channel_id=1, source_target_pairs={{0,4},{4,8},{8,12},{12,16},{16,20},{20,24},{24,28},{1,5},{5,9},{9,... | collective-permute-start | bytes 56 | tf_op jit(solution)/shard_map/while/body/eval_jaxpr/ppermute | solution.py:10
  24.0 8.1 %collective-permute-start = (f32[4,128,128]{1,2,0:T(8,128)S(1)}, f32[4,128,128]{1,2,0:T(8,128)S(1)}, u32[]{:S(2)}, u32[]{:S(2)}) collective-permute-start(f32[4,128,128]{1,2,0:T(8,128)S(1)} %convolution_bitcast_fusion.2), channel_id=1, source_target_pairs={{0,4},{4,8},{8,12},{12,16},{16,20},{20,24},{24,28},{1,5},{5,9},{9,... | collective-permute-start | bytes 786440 | tf_op jit(solution)/shard_map/while/body/eval_jaxpr/ppermute | solution.py:10
  25.3 6.8 %collective-permute-start.1 = (f32[4]{0:T(128)S(1)}, f32[4]{0:T(128)S(1)}, u32[]{:S(2)}, u32[]{:S(2)}) collective-permute-start(f32[4]{0:T(128)S(1)} %get-tuple-element.140), channel_id=1, source_target_pairs={{0,4},{4,8},{8,12},{12,16},{16,20},{20,24},{24,28},{1,5},{5,9},{9,... | collective-permute-start | bytes 56 | tf_op jit(solution)/shard_map/while/body/eval_jaxpr/ppermute | solution.py:10
  36.0 7.7 %collective-permute-start = (f32[4,128,128]{1,2,0:T(8,128)S(1)}, f32[4,128,128]{1,2,0:T(8,128)S(1)}, u32[]{:S(2)}, u32[]{:S(2)}) collective-permute-start(f32[4,128,128]{1,2,0:T(8,128)S(1)} %convolution_bitcast_fusion.2), channel_id=1, source_target_pairs={{0,4},{4,8},{8,12},{12,16},{16,20},{20,24},{24,28},{1,5},{5,9},{9,... | collective-permute-start | bytes 786440 | tf_op jit(solution)/shard_map/while/body/eval_jaxpr/ppermute | solution.py:10
  37.3 6.4 %collective-permute-start.1 = (f32[4]{0:T(128)S(1)}, f32[4]{0:T(128)S(1)}, u32[]{:S(2)}, u32[]{:S(2)}) collective-permute-start(f32[4]{0:T(128)S(1)} %get-tuple-element.140), channel_id=1, source_target_pairs={{0,4},{4,8},{8,12},{12,16},{16,20},{20,24},{24,28},{1,5},{5,9},{9,... | collective-permute-start | bytes 56 | tf_op jit(solution)/shard_map/while/body/eval_jaxpr/ppermute | solution.py:10
  47.5 8.1 %collective-permute-start = (f32[4,128,128]{1,2,0:T(8,128)S(1)}, f32[4,128,128]{1,2,0:T(8,128)S(1)}, u32[]{:S(2)}, u32[]{:S(2)}) collective-permute-start(f32[4,128,128]{1,2,0:T(8,128)S(1)} %convolution_bitcast_fusion.2), channel_id=1, source_target_pairs={{0,4},{4,8},{8,12},{12,16},{16,20},{20,24},{24,28},{1,5},{5,9},{9,... | collective-permute-start | bytes 786440 | tf_op jit(solution)/shard_map/while/body/eval_jaxpr/ppermute | solution.py:10
  48.8 6.8 %collective-permute-start.1 = (f32[4]{0:T(128)S(1)}, f32[4]{0:T(128)S(1)}, u32[]{:S(2)}, u32[]{:S(2)}) collective-permute-start(f32[4]{0:T(128)S(1)} %get-tuple-element.140), channel_id=1, source_target_pairs={{0,4},{4,8},{8,12},{12,16},{16,20},{20,24},{24,28},{1,5},{5,9},{9,... | collective-permute-start | bytes 56 | tf_op jit(solution)/shard_map/while/body/eval_jaxpr/ppermute | solution.py:10
  59.5 8.1 %collective-permute-start = (f32[4,128,128]{1,2,0:T(8,128)S(1)}, f32[4,128,128]{1,2,0:T(8,128)S(1)}, u32[]{:S(2)}, u32[]{:S(2)}) collective-permute-start(f32[4,128,128]{1,2,0:T(8,128)S(1)} %convolution_bitcast_fusion.2), channel_id=1, source_target_pairs={{0,4},{4,8},{8,12},{12,16},{16,20},{20,24},{24,28},{1,5},{5,9},{9,... | collective-permute-start | bytes 786440 | tf_op jit(solution)/shard_map/while/body/eval_jaxpr/ppermute | solution.py:10
  60.8 6.8 %collective-permute-start.1 = (f32[4]{0:T(128)S(1)}, f32[4]{0:T(128)S(1)}, u32[]{:S(2)}, u32[]{:S(2)}) collective-permute-start(f32[4]{0:T(128)S(1)} %get-tuple-element.140), channel_id=1, source_target_pairs={{0,4},{4,8},{8,12},{12,16},{16,20},{20,24},{24,28},{1,5},{5,9},{9,... | collective-permute-start | bytes 56 | tf_op jit(solution)/shard_map/while/body/eval_jaxpr/ppermute | solution.py:10
  71.4 8.1 %collective-permute-start = (f32[4,128,128]{1,2,0:T(8,128)S(1)}, f32[4,128,128]{1,2,0:T(8,128)S(1)}, u32[]{:S(2)}, u32[]{:S(2)}) collective-permute-start(f32[4,128,128]{1,2,0:T(8,128)S(1)} %convolution_bitcast_fusion.2), channel_id=1, source_target_pairs={{0,4},{4,8},{8,12},{12,16},{16,20},{20,24},{24,28},{1,5},{5,9},{9,... | collective-permute-start | bytes 786440 | tf_op jit(solution)/shard_map/while/body/eval_jaxpr/ppermute | solution.py:10
  72.7 6.8 %collective-permute-start.1 = (f32[4]{0:T(128)S(1)}, f32[4]{0:T(128)S(1)}, u32[]{:S(2)}, u32[]{:S(2)}) collective-permute-start(f32[4]{0:T(128)S(1)} %get-tuple-element.140), channel_id=1, source_target_pairs={{0,4},{4,8},{8,12},{12,16},{16,20},{20,24},{24,28},{1,5},{5,9},{9,... | collective-permute-start | bytes 56 | tf_op jit(solution)/shard_map/while/body/eval_jaxpr/ppermute | solution.py:10
  83.3 8.1 %collective-permute-start = (f32[4,128,128]{1,2,0:T(8,128)S(1)}, f32[4,128,128]{1,2,0:T(8,128)S(1)}, u32[]{:S(2)}, u32[]{:S(2)}) collective-permute-start(f32[4,128,128]{1,2,0:T(8,128)S(1)} %convolution_bitcast_fusion.2), channel_id=1, source_target_pairs={{0,4},{4,8},{8,12},{12,16},{16,20},{20,24},{24,28},{1,5},{5,9},{9,... | collective-permute-start | bytes 786440 | tf_op jit(solution)/shard_map/while/body/eval_jaxpr/ppermute | solution.py:10
  84.6 6.8 %collective-permute-start.1 = (f32[4]{0:T(128)S(1)}, f32[4]{0:T(128)S(1)}, u32[]{:S(2)}, u32[]{:S(2)}) collective-permute-start(f32[4]{0:T(128)S(1)} %get-tuple-element.140), channel_id=1, source_target_pairs={{0,4},{4,8},{8,12},{12,16},{16,20},{20,24},{24,28},{1,5},{5,9},{9,... | collective-permute-start | bytes 56 | tf_op jit(solution)/shard_map/while/body/eval_jaxpr/ppermute | solution.py:10
  120.0 7.9 %copy-start = (bf16[1,4,128,128]{3,2,1,0:T(8,128)(2,1)S(1)}, bf16[1,4,128,128]{3,2,1,0:T(8,128)(2,1)}, u32[]{:S(2)}) copy-start(bf16[1,4,128,128]{3,2,1,0:T(8,128)(2,1)} %param.11) | copy-start | bytes 393220
  151.4 68.4 %reduce-scatter.2.cloned.1.call-start = ((), (), s32[]{:S(2)}) async-start(), calls=%async_computation.2 | async-start | bytes 655360 | tf_op jit(solution)/shard_map/reduce_scatter | solution.py:74
Sparse Core Ops, SparseCore 0:
  151.5 33.5 all-reduce.2
  197.1 22.5 reduce-scatter.1
where the time goes:
time: 229 us; the launch traced here: 227 us
  waiting for transfers between devices  93.7 us (41%)
  matrix products  35.8 us (16%)
  local copies, waits for them, and re-layouts  30.9 us (13%)
  blocking collectives  28.3 us (12%)
  starting transfers between devices  18.3 us (8%)
  between operations  15.5 us (7%)
  other arithmetic  3.56 us (2%)
    ppermute x14, waiting for transfers between devices, shifted(): return lax.ppermute(array, axis, pairs)  39 us
    psum x1, waiting for transfers between devices, on_device(): lax.psum(partial_sum.astype(jnp.bfloat16), 'op').astype(jnp.float32)  33.5 us
    reduce_scatter x1, waiting for transfers between devices, on_device(): lax.psum_scatter(second_part.astype(jnp.bfloat16), 'op', scatter_dimensio...  21.1 us
    dot_general x2, matrix products, apply_ham(): jnp.einsum('kpil,kpml->pim', half_prod, right_local, preferred_element_ty...  18.7 us
    ppermute x14, starting transfers between devices, shifted(): return lax.ppermute(array, axis, pairs)  18.1 us
    unnamed x1, blocking collectives  13.1 us
    gather x7, local copies, waits for them, and re-layouts, relay_step(): jnp.take(own_blocks, current, axis=0)  12.5 us
    gather x7, local copies, waits for them, and re-layouts, relay_step(): next_labels = jnp.take(sector_map, current).astype(jnp.float32)  9.07 us
  transfers between devices with their start and end apart: 16, of which 9 were waited for; matrix products, arithmetic and copies ran while one was open for 1% of the time, Pallas kernels for 0%

commit v1 on v0

v1 whole, which is shorter than its diff:
```python
import functools

import jax
import jax.numpy as jnp
from jax import lax
from jax.experimental import pallas as pl
from jax.experimental.pallas import tpu as pltpu
from jax.sharding import PartitionSpec as P

MESH = pl.DeviceIdType.MESH
F32 = jnp.float32
BF16 = jnp.bfloat16
NT = (((1,), (1,)), ((), ()))
TN = (((0,), (0,)), ((), ()))


def mixed(index, off, count):
    out = index * 0
    bit = 1
    while bit < count:
        digit = (index // bit) % 2
        out = out + bit * ((1 - digit) if off & bit else digit)
        bit *= 2
    return out


def split(value):
    high = value.astype(BF16)
    return high, (value - high.astype(F32)).astype(BF16)


def mm(a, b):
    return jnp.dot(a, b, preferred_element_type=F32)


def kernel(
    segs, groups, label_ref, site_hbm, left_hbm, right_hbm, wave_hbm, out1_ref, out2_ref,
    site, left, right, wave, lab_own, lab_all, lab_smem, sector_to, sector_from,
    prefix, step_hi, step_lo, step_out, hpsi, z_own, zs1, zr1, zs2, zr2,
    load_sem, smem_sem, lab_send, lab_recv, wave_send, wave_recv, chain_send, chain_recv,
    pre_send, pre_recv, z1_send, z1_recv, h_send, h_recv, z2_send, z2_recv,
):
    seg = lax.axis_index("seg")
    me = lax.axis_index("op")
    sectors, block_len = prefix.shape[0], prefix.shape[1]
    per = sectors // groups
    ops = left.shape[0]
    first = me * per

    loads = [
        pltpu.make_async_copy(site_hbm.at[0], site, load_sem.at[0]),
        pltpu.make_async_copy(wave_hbm.at[0], wave.at[pl.ds(first, per)], load_sem.at[1]),
        pltpu.make_async_copy(left_hbm, left, load_sem.at[2]),
        pltpu.make_async_copy(right_hbm.at[0], right, load_sem.at[3]),
    ]
    for load in loads:
        load.start()
    lab_own[...] = jnp.zeros_like(lab_own)
    lab_own[0:1, 0:sectors] = label_ref[...]
    lab_all[seg] = lab_own[...]

    barrier = pltpu.get_barrier_semaphore()
    for off in range(1, groups):
        pl.semaphore_signal(
            barrier, inc=1, device_id={"op": mixed(me, off, groups)}, device_id_type=MESH
        )
    for off in range(1, segs):
        pl.semaphore_signal(
            barrier, inc=1, device_id={"seg": (seg + off) % segs}, device_id_type=MESH
        )
    pl.semaphore_wait(barrier, groups + segs - 2)

    def to_op(src, dst, send, recv, off):
        return pltpu.make_async_remote_copy(
            src_ref=src, dst_ref=dst, send_sem=send, recv_sem=recv,
            device_id={"op": mixed(me, off, groups)}, device_id_type=MESH,
        )

    def lab_copy(off, source):
        return pltpu.make_async_remote_copy(
            src_ref=lab_own, dst_ref=lab_all.at[source], send_sem=lab_send.at[off - 1],
            recv_sem=lab_recv.at[off - 1],
            device_id={"seg": (seg + off) % segs}, device_id_type=MESH,
        )

    for off in range(1, segs):
        lab_copy(off, seg).start()

    loads[1].wait()

    def wave_copy(off, owner):
        rows = pl.ds(owner * per, per)
        return to_op(
            wave.at[rows], wave.at[rows], wave_send.at[off - 1], wave_recv.at[off - 1], off
        )

    for off in range(1, groups):
        wave_copy(off, me).start()

    for off in range(1, segs):
        lab_copy(off, (seg + segs - off) % segs).wait_recv()
    to_smem = pltpu.make_async_copy(lab_all, lab_smem, smem_sem)
    to_smem.start()
    to_smem.wait()

    def reached(q, _):
        p = lax.fori_loop(0, seg, lambda s, p: lab_smem[s, 0, p], q)
        sector_to[q] = jnp.clip(p, 0, sectors - 1)
        return 0

    lax.fori_loop(0, sectors, reached, 0)

    loads[0].wait()
    for j in range(per):
        high, low = split(site[sector_to[first + j]])
        step_hi[j] = high
        step_lo[j] = low

    def chain_copy(j):
        return pltpu.make_async_remote_copy(
            src_ref=step_out.at[j], dst_ref=prefix.at[first + j], send_sem=chain_send.at[j],
            recv_sem=chain_recv.at[j],
            device_id={"seg": (seg + 1) % segs}, device_id_type=MESH,
        )

    def prefix_copy(off, j, owner):
        block = prefix.at[owner * per + j]
        return to_op(block, block, pre_send.at[off - 1, j], pre_recv.at[off - 1, j], off)

    row = lax.broadcasted_iota(jnp.int32, (block_len, block_len), 0)
    col = lax.broadcasted_iota(jnp.int32, (block_len, block_len), 1)
    for j in range(per):

        @pl.when(seg == 0)
        def _():
            prefix[first + j] = jnp.where(row == col, 1.0, 0.0).astype(BF16)

        @pl.when(seg > 0)
        def _():
            chain_copy(j).wait_recv()

        @pl.when(seg < segs - 1)
        def _():
            block = prefix[first + j]
            step_out[j] = (mm(block, step_hi[j]) + mm(block, step_lo[j])).astype(BF16)
            chain_copy(j).start()

        for off in range(1, groups):
            prefix_copy(off, j, me).start()

    def found(p, _):
        def look(q, at):
            return jnp.where(sector_to[q] == p, q, at)

        sector_from[p] = lax.fori_loop(0, sectors, look, jnp.int32(0))
        return 0

    lax.fori_loop(0, sectors, found, 0)

    for off in range(1, groups):
        wave_copy(off, mixed(me, off, groups)).wait_recv()
        for j in range(per):
            prefix_copy(off, j, mixed(me, off, groups)).wait_recv()
    loads[2].wait()
    loads[3].wait()

    def terms(q, p, vector):
        inner = mm(prefix[q], vector).astype(BF16)
        total = jnp.zeros((block_len, block_len), F32)
        for k in range(0, ops, 2):
            pair = [k] if k + 1 == ops else [k, k + 1]
            half = [mm(left[i, q], inner).astype(BF16) for i in pair]
            other = [right[i, p] for i in pair]
            total += lax.dot_general(
                jnp.concatenate(half, axis=1), jnp.concatenate(other, axis=1), NT,
                preferred_element_type=F32,
            )
        return total

    def z1_copy(off, j):
        return to_op(
            zs1.at[off - 1, j], zr1.at[off - 1, j],
            z1_send.at[off - 1, j], z1_recv.at[off - 1, j], off,
        )

    def z2_copy(off, j):
        return to_op(
            zs2.at[off - 1, j], zr2.at[off - 1, j],
            z2_send.at[off - 1, j], z2_recv.at[off - 1, j], off,
        )

    for off in range(groups):
        owner = mixed(me, off, groups)

        def first_step(j, _):
            q = owner * per + j
            p = sector_to[q]
            total = terms(q, p, wave[p])
            if off:
                zs1[off - 1, j] = total.astype(BF16)
                z1_copy(off, j).start()
            else:
                z_own[j] = total
            return 0

        lax.fori_loop(0, per, first_step, 0)

    def back(q, total):
        high, low = split(total)
        block = prefix[q]
        return lax.dot_general(block, high, TN, preferred_element_type=F32) + lax.dot_general(
            block, low, TN, preferred_element_type=F32
        )

    def h_copy(off, j, owner):
        block = hpsi.at[owner * per + j]
        return to_op(block, block, h_send.at[off - 1, j], h_recv.at[off - 1, j], off)

    for j in range(per):
        total = z_own[j]
        for off in range(1, groups):
            z1_copy(off, j).wait_recv()
            total += zr1[off - 1, j].astype(F32)
        hpsi[first + j] = back(first + j, total).astype(BF16)
        for off in range(1, groups):
            h_copy(off, j, me).start()
    for j in range(per):
        for off in range(1, groups):
            h_copy(off, j, mixed(me, off, groups)).wait_recv()

    for off in list(range(1, groups)) + [0]:
        owner = mixed(me, off, groups)

        def second_step(j, _):
            p = owner * per + j
            q = sector_from[p]
            total = terms(q, p, hpsi[q])
            if off:
                zs2[off - 1, j] = total.astype(BF16)
                z2_copy(off, j).start()
            else:
                z_own[j] = total
            return 0

        lax.fori_loop(0, per, second_step, 0)

    def add_squares(q, sums):
        block = hpsi[q].astype(F32)
        return sums + block * block

    squares = lax.fori_loop(0, sectors, add_squares, jnp.zeros((block_len, block_len), F32))
    entries = sectors * block_len * block_len
    scale = lax.rsqrt(jnp.sum(squares, keepdims=True) / entries + 1e-06)
    for j in range(per):
        out1_ref[0, j] = hpsi[sector_from[first + j]]
    for j in range(per):
        total = z_own[j]
        for off in range(1, groups):
            z2_copy(off, j).wait_recv()
            total += zr2[off - 1, j].astype(F32)
        out2_ref[0, j] = (back(sector_from[first + j], total) * scale).astype(BF16)

    for off in range(1, segs):
        lab_copy(off, seg).wait_send()
    for off in range(1, groups):
        wave_copy(off, me).wait_send()
        for j in range(per):
            prefix_copy(off, j, me).wait_send()
            z1_copy(off, j).wait_send()
            h_copy(off, j, me).wait_send()
            z2_copy(off, j).wait_send()

    @pl.when(seg < segs - 1)
    def _():
        for j in range(per):
            chain_copy(j).wait_send()


def on_device(label_map, site_blocks, left_ops, right_ops, wavefunction):
    segs, groups = lax.axis_size("seg"), lax.axis_size("op")
    sectors, n = site_blocks.shape[1], site_blocks.shape[2]
    ops = left_ops.shape[0]
    per = sectors // groups
    dma = pltpu.SemaphoreType.DMA
    peers = groups - 1
    blocks = lambda *lead, dtype=BF16: pltpu.VMEM(lead + (n, n), dtype)
    out = jax.ShapeDtypeStruct((1, per, n, n), BF16)
    vmem = pl.BlockSpec(memory_space=pltpu.VMEM)
    hbm = pl.BlockSpec(memory_space=pl.ANY)
    return pl.pallas_call(
        functools.partial(kernel, segs, groups),
        out_shape=(out, out),
        in_specs=[vmem, hbm, hbm, hbm, hbm],
        out_specs=(vmem, vmem),
        scratch_shapes=[
            blocks(sectors, dtype=F32), blocks(ops, sectors), blocks(ops, sectors),
            blocks(sectors),
            pltpu.VMEM((8, 128), jnp.int32), pltpu.VMEM((segs, 8, 128), jnp.int32),
            pltpu.SMEM((segs, 8, 128), jnp.int32),
            pltpu.SMEM((sectors,), jnp.int32), pltpu.SMEM((sectors,), jnp.int32),
            blocks(sectors), blocks(per), blocks(per), blocks(per), blocks(sectors),
            blocks(per, dtype=F32),
            blocks(peers, per), blocks(peers, per), blocks(peers, per), blocks(peers, per),
            dma((4,)), dma, dma((segs - 1,)), dma((segs - 1,)), dma((peers,)), dma((peers,)),
            dma((per,)), dma((per,)),
            dma((peers, per)), dma((peers, per)), dma((peers, per)), dma((peers, per)),
            dma((peers, per)), dma((peers, per)), dma((peers, per)), dma((peers, per)),
        ],
        compiler_params=pltpu.CompilerParams(
            collective_id=0, has_side_effects=True, vmem_limit_bytes=56 * 1024 * 1024
        ),
    )(label_map, site_blocks, left_ops, right_ops, wavefunction)


def solution(mesh):
    in_specs = (
        P("seg", None),
        P("seg", None, None, None),
        P("op", None, None, None),
        P("seg", "op", None, None, None),
        P("seg", "op", None, None),
    )
    out_specs = (P("seg", "op", None, None), P("seg", "op", None, None))
    return jax.shard_map(
        on_device, mesh=mesh, in_specs=in_specs, out_specs=out_specs, check_vma=False
    )
```

time: 229 us -> 71.4 us (0.31); the launches traced: 227 us -> 71.3 us
  waiting for transfers between devices: 93.7 us -> 0 us
  Pallas kernels: 0 us -> 67.5 us
  matrix products: 35.8 us -> 0 us
  blocking collectives: 28.3 us -> 0 us
  local copies, waits for them, and re-layouts: 30.9 us -> 3.14 us
  starting transfers between devices: 18.3 us -> 0 us
  between operations: 15.5 us -> 0.64 us
  other arithmetic: 3.56 us -> 0 us
    pallas_call x0 -> x1, Pallas kernels: none -> 67.5 us  [on_device(): pl.pallas_call(functools.partial(kernel, segs, groups), out_shape=(out, o...]
    ppermute x14 -> x0, waiting for transfers between devices: 39 us -> none  [shifted(): return lax.ppermute(array, axis, pairs)]
    dot_general x11 -> x0, matrix products: 35.8 us -> none  [the longest x2 18.7 us: apply_ham(): jnp.einsum('kpil,kpml->pim', half_prod, right_local, preferred_element_ty...]
    psum x1 -> x0, waiting for transfers between devices: 33.5 us -> none  [on_device(): lax.psum(partial_sum.astype(jnp.bfloat16), 'op').astype(jnp.float32)]
    gather x15 -> x0, local copies, waits for them, and re-layouts: 28.4 us -> none  [the longest x7 12.5 us: relay_step(): jnp.take(own_blocks, current, axis=0)]
    reduce_scatter x1 -> x0, waiting for transfers between devices: 21.1 us -> none  [on_device(): lax.psum_scatter(second_part.astype(jnp.bfloat16), 'op', scatter_dimensio...]
    ppermute x14 -> x0, starting transfers between devices: 18.1 us -> none  [shifted(): return lax.ppermute(array, axis, pairs)]
    all_gather x2 -> x0, blocking collectives: 15.2 us -> none  [the longest x1 7.9 us: on_device(): lax.all_gather(relayed[0].astype(jnp.bfloat16), 'op', axis=0, tiled=True)]
  transfers between devices with their start and end apart: 16 -> 0, of which waited for: 9 -> 0; matrix products, arithmetic and copies ran while one was open for 1% -> 0% of each run, Pallas kernels for 0% -> 0%
where the time goes in v1:
time: 71.4 us; the launch traced here: 71.3 us
  Pallas kernels  67.5 us (95%)
  local copies, waits for them, and re-layouts  3.14 us (4%)
    pallas_call x1, Pallas kernels, on_device(): pl.pallas_call(functools.partial(kernel, segs, groups), out_shape=(out, o...  67.5 us
    unnamed x2, local copies, waits for them, and re-layouts  3.14 us

profile of v1, /device:TPU:29, one launch (start us, length us, event | category | flops | bytes accessed | tf_op | source)
XLA Modules:
  0.0 71.3 jit_solution(11240419891440181608)
XLA Ops:
  0.6 67.5 %shard_map.68 = (bf16[1,4,128,128]{3,2,1,0:T(8,128)(2,1)}, bf16[1,4,128,128]{3,2,1,0:T(8,128)(2,1)}) custom-call(s32[1,16]{1,0:T(1,128)} %label_ref.1, f32[1,16,128,128]{3,2,1,0:T(8,128)} %site_hbm.1, bf16[12,16,128,128]{3,2,1,0:T(8,128)(2,1)} %left_hbm.1, bf16[1,12,16,128,128]{4,3,2,1,0:T(8,128)(2,1)} %right_hbm.1, bf16[1,4,128,128]{3,2,1,0:T(8,128)(2,1)} %wave_hbm.1), custom_call_target="tpu_custom_call" | custom-call | tf_op jit(solution)/shard_map/pallas_call | solution.py:290
  68.1 1.6 %copy.9 = bf16[1,4,128,128]{3,2,1,0:T(8,128)(2,1)} copy(bf16[1,4,128,128]{3,2,1,0:T(8,128)(2,1)} %get-tuple-element.4) | data formatting | bytes 262144
  69.7 1.6 %copy.10 = bf16[1,4,128,128]{3,2,1,0:T(8,128)(2,1)} copy(bf16[1,4,128,128]{3,2,1,0:T(8,128)(2,1)} %get-tuple-element.5) | data formatting | bytes 262144

commit v2 on v1

--- a/solution.py
+++ b/solution.py
@@ -159,23 +159,18 @@
 
     for off in range(1, groups):
         wave_copy(off, mixed(me, off, groups)).wait_recv()
-        for j in range(per):
-            prefix_copy(off, j, mixed(me, off, groups)).wait_recv()
     loads[2].wait()
     loads[3].wait()
 
     def terms(q, p, vector):
         inner = mm(prefix[q], vector).astype(BF16)
-        total = jnp.zeros((block_len, block_len), F32)
-        for k in range(0, ops, 2):
-            pair = [k] if k + 1 == ops else [k, k + 1]
-            half = [mm(left[i, q], inner).astype(BF16) for i in pair]
-            other = [right[i, p] for i in pair]
-            total += lax.dot_general(
-                jnp.concatenate(half, axis=1), jnp.concatenate(other, axis=1), NT,
-                preferred_element_type=F32,
-            )
-        return total
+        stacked = left[:, q].reshape(ops * block_len, block_len)
+        half = mm(stacked, inner).astype(BF16).reshape(ops, block_len, block_len)
+        return lax.dot_general(
+            jnp.concatenate([half[k] for k in range(ops)], axis=1),
+            jnp.concatenate([right[k, p] for k in range(ops)], axis=1),
+            NT, preferred_element_type=F32,
+        )
 
     def z1_copy(off, j):
         return to_op(
@@ -189,21 +184,23 @@
             z2_send.at[off - 1, j], z2_recv.at[off - 1, j], off,
         )
 
-    for off in range(groups):
+    for j in range(per):
+        p = sector_to[first + j]
+        z_own[j] = terms(first + j, p, wave[p])
+    for off in range(1, groups):
+        for j in range(per):
+            prefix_copy(off, j, mixed(me, off, groups)).wait_recv()
+    for off in range(1, groups):
         owner = mixed(me, off, groups)
-
-        def first_step(j, _):
-            q = owner * per + j
-            p = sector_to[q]
-            total = terms(q, p, wave[p])
-            if off:
-                zs1[off - 1, j] = total.astype(BF16)
-                z1_copy(off, j).start()
-            else:
-                z_own[j] = total
-            return 0
-
-        lax.fori_loop(0, per, first_step, 0)
+        for j in range(0, per, 2):
+            totals = []
+            for i in range(j, j + 2):
+                q = owner * per + i
+                p = sector_to[q]
+                totals.append(terms(q, p, wave[p]))
+            for i in range(j, j + 2):
+                zs1[off - 1, i] = totals[i - j].astype(BF16)
+                z1_copy(off, i).start()
 
     def back(q, total):
         high, low = split(total)
@@ -231,18 +228,18 @@
     for off in list(range(1, groups)) + [0]:
         owner = mixed(me, off, groups)
 
-        def second_step(j, _):
-            p = owner * per + j
-            q = sector_from[p]
-            total = terms(q, p, hpsi[q])
-            if off:
-                zs2[off - 1, j] = total.astype(BF16)
-                z2_copy(off, j).start()
-            else:
-                z_own[j] = total
-            return 0
-
-        lax.fori_loop(0, per, second_step, 0)
+        for j in range(0, per, 2):
+            totals = []
+            for i in range(j, j + 2):
+                p = owner * per + i
+                q = sector_from[p]
+                totals.append(terms(q, p, hpsi[q]))
+            for i in range(j, j + 2):
+                if off:
+                    zs2[off - 1, i] = totals[i - j].astype(BF16)
+                    z2_copy(off, i).start()
+                else:
+                    z_own[i] = totals[i - j]
 
     def add_squares(q, sums):
         block = hpsi[q].astype(F32)

time: 71.4 us -> 67.5 us (0.945)
  Pallas kernels: 67.5 us -> 63.6 us
    pallas_call x1, Pallas kernels: 67.5 us -> 63.6 us  [on_device(): pl.pallas_call(functools.partial(kernel, segs, groups), out_shape=(out, o...]
where the time goes in v2:
time: 67.5 us; the launch traced here: 67.4 us
  Pallas kernels  63.6 us (94%)
  local copies, waits for them, and re-layouts  3.14 us (5%)
    pallas_call x1, Pallas kernels, on_device(): pl.pallas_call(functools.partial(kernel, segs, groups), out_shape=(out, o...  63.6 us
    unnamed x2, local copies, waits for them, and re-layouts  3.14 us

profile of v2, /device:TPU:29, one launch (start us, length us, event | category | flops | bytes accessed | tf_op | source)
XLA Modules:
  0.0 67.4 jit_solution(14151772257258733180)
XLA Ops:
  0.6 63.6 %shard_map.68 = (bf16[1,4,128,128]{3,2,1,0:T(8,128)(2,1)}, bf16[1,4,128,128]{3,2,1,0:T(8,128)(2,1)}) custom-call(s32[1,16]{1,0:T(1,128)} %label_ref.1, f32[1,16,128,128]{3,2,1,0:T(8,128)} %site_hbm.1, bf16[12,16,128,128]{3,2,1,0:T(8,128)(2,1)} %left_hbm.1, bf16[1,12,16,128,128]{4,3,2,1,0:T(8,128)(2,1)} %right_hbm.1, bf16[1,4,128,128]{3,2,1,0:T(8,128)(2,1)} %wave_hbm.1), custom_call_target="tpu_custom_call" | custom-call | tf_op jit(solution)/shard_map/pallas_call | solution.py:287
  64.2 1.6 %copy.9 = bf16[1,4,128,128]{3,2,1,0:T(8,128)(2,1)} copy(bf16[1,4,128,128]{3,2,1,0:T(8,128)(2,1)} %get-tuple-element.4) | data formatting | bytes 262144
  65.8 1.6 %copy.10 = bf16[1,4,128,128]{3,2,1,0:T(8,128)(2,1)} copy(bf16[1,4,128,128]{3,2,1,0:T(8,128)(2,1)} %get-tuple-element.5) | data formatting | bytes 262144
